TPU v7x, 32 devices: a whole 2x2x4 slice. The times are simulated.
32 devices in a mesh: groups: 2 (over y), prob: 16 (over z, x, core).
Axes of the slice: x: 2, y: 2, z: 4, core: 2. Of those that a mesh axis runs over, the one named last changes fastest.
Arguments:
- segment_queries: bfloat16 [32, 4, 64, 8192], P(('groups', 'prob')), parts along dimension 0, may hold values from -18 to 18
- segment_kv: bfloat16 [32, 4, 2, 64, 1024], P(('groups', 'prob')), parts along dimension 0, may hold values from -18 to 18
- prefix_kv: bfloat16 [32, 2, 256, 1024], P(('groups', 'prob')), parts along dimension 0, may hold values from -6 to 6
- page_pool: bfloat16 [2048, 2, 8, 1024], P(('groups', 'prob')), parts along dimension 0, may hold values from -6 to 6
- beam_count: int32 [32], P(('groups', 'prob')), parts along dimension 0, may hold values from 1 to 4, as said below
- page_version: int32 [32, 4, 16], P(('groups', 'prob')), parts along dimension 0, may hold values from 0 to 3, as said below
- page_slot: int32 [32, 16, 4], P(('groups', 'prob')), parts along dimension 0, may hold values from 0 to 63, as said below
Outputs:
- attention_out: bfloat16 [32, 4, 64, 8192], P(('groups', 'prob')), parts along dimension 0
There are 2 independent parts, one for each index of `groups`. A program takes and returns all parts, laid end to end along the dimension named above; each array names one. Nothing has to cross between parts.
Inputs may be any that keep to these rules, and one draw needn't show every extreme that they name: `beam_count`: live beams of each problem; some problem has 4 in every draw. `page_version`: beam 0 reads version 0 of every page; every other beam b reads the versions of an earlier beam of its problem up to some page and version b from there on, its last page always version b. Version v of context page j of problem p is page_pool row d * 64 + page_slot[p, j, v] with d = (p + 1 + j * 4 + v) mod 16; every pool row is named by exactly one (p, j, v).
All inputs are finite; a program needn't handle non-finite values.
Results may differ from a plain program's by a relative error of at most 0.007.
Values may be sent and summed in bfloat16 or wider, within the bound.
A program may use at most 128 MiB of HBM per device.

v0:
```python
import functools
import math

import jax
import jax.numpy as jnp
import numpy as np
from jax import lax
from jax.experimental import pallas as pl
from jax.experimental.pallas import tpu as pltpu
from jax.sharding import PartitionSpec as P

HD = 128
NEG_FILL = -1e30
LOG2_SCALE = math.log2(math.e) / math.sqrt(HD)


def rotary_tables(length, offset):
    half = HD // 2
    frequency = np.exp(np.arange(half) * (-2.0 * math.log(1000000.0) / HD))
    angles = (np.arange(length) + offset)[:, None] * frequency[None, :]
    cosine, sine = np.cos(angles), np.sin(angles)
    return (
        jnp.asarray(np.concatenate([cosine, cosine], axis=1), jnp.float32),
        jnp.asarray(np.concatenate([-sine, sine], axis=1), jnp.float32),
    )


def rotate(values, cosine, signed_sine):
    floats = values.astype(jnp.float32)
    swapped = pltpu.roll(floats, HD // 2, 1)
    return (floats * cosine + swapped * signed_sine).astype(jnp.bfloat16)


def dot_keys(queries, keys):
    return lax.dot_general(
        queries, keys, (((1,), (1,)), ((), ())), preferred_element_type=jnp.float32
    )


def dot_values(weights, values):
    extended = jnp.concatenate([values, jnp.ones_like(values)], axis=1)
    return jnp.dot(weights, extended, preferred_element_type=jnp.float32)


def local_part(q_ref, seg_ref, prefix_ref, cos_ref, sin_ref, rot_ref, acc_ref, ml_ref):
    seg_len = q_ref.shape[2]
    kv_heads = rot_ref.shape[1]
    group = q_ref.shape[3] // HD // kv_heads
    rows = group * seg_len
    cosine, sine = cos_ref[...], sin_ref[...]
    token = lax.broadcasted_iota(jnp.int32, (group, seg_len, seg_len), 1).reshape(rows, seg_len)
    key = lax.broadcasted_iota(jnp.int32, (rows, seg_len), 1)
    causal = token >= key
    lane = lax.broadcasted_iota(jnp.int32, (rows, HD), 1)
    for head in range(kv_heads):
        queries = jnp.concatenate(
            [
                rotate(q_ref[0, 0, :, pl.ds((head * group + g) * HD, HD)], cosine, sine)
                for g in range(group)
            ],
            axis=0,
        )
        columns = pl.ds(head * HD, HD)
        fresh_keys = rotate(seg_ref[0, 0, 0, :, columns], cosine, sine)
        prefix_scores = dot_keys(queries, prefix_ref[0, 0, :, columns])
        fresh_scores = jnp.where(causal, dot_keys(queries, fresh_keys), NEG_FILL)
        row_max = jnp.maximum(
            prefix_scores.max(-1, keepdims=True), fresh_scores.max(-1, keepdims=True)
        )
        shift = row_max * LOG2_SCALE
        prefix_exp = jnp.exp2(prefix_scores * LOG2_SCALE - shift).astype(jnp.bfloat16)
        fresh_exp = jnp.exp2(fresh_scores * LOG2_SCALE - shift).astype(jnp.bfloat16)
        mixed = dot_values(prefix_exp, prefix_ref[0, 1, :, columns]) + dot_values(
            fresh_exp, seg_ref[0, 0, 1, :, columns]
        )
        rot_ref[0, head] = queries
        acc_ref[0, head] = mixed[:, :HD]
        ml_ref[0, head] = jnp.where(lane < HD // 2, shift, mixed[:, HD:])


def paged_part(
    index_ref, count_ref, rot_ref, acc_ref, ml_ref, pages_ref, out_ref
):
    beam = pl.program_id(0)
    kv_heads = rot_ref.shape[1]
    seg_len = out_ref.shape[2]
    group = out_ref.shape[3] // HD // kv_heads
    pages = index_ref.shape[1]
    live = beam < count_ref[0]
    for head in range(kv_heads):
        columns = pl.ds(head * HD, HD)

        def gathered(which):
            return jnp.concatenate(
                [
                    pages_ref[index_ref[beam, j], which, :, columns].astype(jnp.float32)
                    for j in range(pages)
                ],
                axis=0,
            ).astype(jnp.bfloat16)

        scores = dot_keys(rot_ref[0, head], gathered(0)) * LOG2_SCALE
        packed = ml_ref[0, head]
        old_shift, old_total = packed[:, :1], packed[:, HD - 1 :]
        shift = jnp.maximum(old_shift, scores.max(-1, keepdims=True))
        weights = jnp.exp2(scores - shift).astype(jnp.bfloat16)
        decay = jnp.exp2(old_shift - shift)
        mixed = dot_values(weights, gathered(1))
        total = mixed[:, HD:] + old_total * decay
        result = (mixed[:, :HD] + acc_ref[0, head] * decay) / total
        result = jnp.where(live, result, 0.0).astype(jnp.bfloat16)
        for g in range(group):
            out_ref[0, 0, :, pl.ds((head * group + g) * HD, HD)] = result[
                g * seg_len : (g + 1) * seg_len
            ]


def per_device(
    segment_queries, segment_kv, prefix_kv, page_pool, beam_count, page_version, page_slot
):
    devices = lax.axis_size("prob")
    myself = lax.axis_index("prob")
    _, beams, seg_len, model_width = segment_queries.shape
    shared = prefix_kv.shape[2]
    pool_pages, _, page_len, kv_width = page_pool.shape
    context_pages = page_version.shape[2]
    kv_heads = kv_width // HD
    rows = model_width // kv_width * seg_len
    capacity = (pool_pages + devices - 1) // devices
    cosine, sine = rotary_tables(seg_len, shared + context_pages * page_len)

    slots = page_slot.reshape(-1)
    slots = jnp.pad(slots, (0, capacity * devices - slots.shape[0]))
    wanted = slots.reshape(capacity, devices).T
    requests = wanted[(jnp.arange(devices) - myself - 1) % devices]
    asked = lax.all_to_all(requests, "prob", split_axis=0, concat_axis=0, tiled=True)
    located = page_pool[asked.reshape(-1)].reshape(devices, capacity, 2, page_len, kv_width)
    received = lax.all_to_all(located, "prob", split_axis=0, concat_axis=0, tiled=True)
    received = received.reshape(devices * capacity, 2, page_len, kv_width)
    copy_index = jnp.arange(context_pages, dtype=jnp.int32)[None, :] * beams + page_version[0]
    index = (myself + 1 + copy_index) % devices * capacity + copy_index // devices

    per_head = lambda b: (b, 0, 0, 0)
    head_block = pl.BlockSpec((1, kv_heads, rows, HD), per_head)
    params = pltpu.CompilerParams(vmem_limit_bytes=48 * 1024 * 1024)
    flops = 4 * beams * kv_heads * rows * HD
    rot, acc, ml = pl.pallas_call(
        local_part,
        grid=(beams,),
        in_specs=[
            pl.BlockSpec((1, 1, seg_len, model_width), lambda b: (0, b, 0, 0)),
            pl.BlockSpec((1, 1, 2, seg_len, kv_width), lambda b: (0, b, 0, 0, 0)),
            pl.BlockSpec((1, 2, shared, kv_width), lambda b: (0, 0, 0, 0)),
            pl.BlockSpec((seg_len, HD), lambda b: (0, 0)),
            pl.BlockSpec((seg_len, HD), lambda b: (0, 0)),
        ],
        out_specs=[head_block, head_block, head_block],
        out_shape=[
            jax.ShapeDtypeStruct((beams, kv_heads, rows, HD), jnp.bfloat16),
            jax.ShapeDtypeStruct((beams, kv_heads, rows, HD), jnp.float32),
            jax.ShapeDtypeStruct((beams, kv_heads, rows, HD), jnp.float32),
        ],
        compiler_params=params,
        cost_estimate=pl.CostEstimate(
            flops=flops * (shared + seg_len),
            bytes_accessed=30 * 1024 * 1024,
            transcendentals=beams * kv_heads * rows * (shared + seg_len),
        ),
        name="local_part",
    )(segment_queries, segment_kv, prefix_kv, cosine, sine)
    grid_spec = pltpu.PrefetchScalarGridSpec(
        num_scalar_prefetch=2,
        grid=(beams,),
        in_specs=[
            pl.BlockSpec((1, kv_heads, rows, HD), lambda b, *_: (b, 0, 0, 0)),
            pl.BlockSpec((1, kv_heads, rows, HD), lambda b, *_: (b, 0, 0, 0)),
            pl.BlockSpec((1, kv_heads, rows, HD), lambda b, *_: (b, 0, 0, 0)),
            pl.BlockSpec(received.shape, lambda b, *_: (0, 0, 0, 0)),
        ],
        out_specs=pl.BlockSpec((1, 1, seg_len, model_width), lambda b, *_: (0, b, 0, 0)),
    )
    return pl.pallas_call(
        paged_part,
        grid_spec=grid_spec,
        out_shape=jax.ShapeDtypeStruct(segment_queries.shape, jnp.bfloat16),
        compiler_params=params,
        name="paged_part",
    )(index, beam_count, rot, acc, ml, received)


def solution(mesh):
    placed = (
        P(("groups", "prob"), None, None, None),
        P(("groups", "prob"), None, None, None, None),
        P(("groups", "prob"), None, None, None),
        P(("groups", "prob"), None, None, None),
        P(("groups", "prob")),
        P(("groups", "prob"), None, None),
        P(("groups", "prob"), None, None),
    )
    return jax.shard_map(
        per_device,
        mesh=mesh,
        in_specs=placed,
        out_specs=P(("groups", "prob"), None, None, None),
        check_vma=False,
    )
```

profile of v0, /device:TPU:11, one launch (start us, length us, event | category | flops | bytes accessed | tf_op | source)
XLA Modules:
  0.0 93.9 jit_solution(14978368473328547264)
XLA Ops:
  0.0 0.0 copy-start
  0.0 0.9 copy.18
  0.9 0.1 reshape.102
  1.0 0.1 copy.19
  1.1 0.6 gather_fusion
  1.7 10.2 %all_to_all.14 = s32[16,1,4]{2,1,0:T(1,128)S(1)} all-to-all(s32[16,1,4]{2,1,0:T(1,128)S(1)} %bitcast.16), channel_id=1, replica_groups=mesh['groups'=2,'prob'=16] {'prob'}, dimensions={0} | all-to-all | bytes 512 | tf_op jit(solution)/shard_map/all_to_all | solution.py:136
  11.8 0.5 broadcast.130
  12.3 0.7 reduce.3
  13.0 0.1 reshape.103
  13.1 0.0 copy-done
  13.1 2.0 %gather_fusion.1 = bf16[64,2,8,1024]{3,2,1,0:T(8,128)(2,1)} fusion(bf16[64,2,8,1024]{3,2,1,0:T(8,128)(2,1)S(1)} %copy-done, s32[1024]{0:T(1024)S(1)} %pad_clamp_fusion), kind=kCustom, calls=%fused_computation.1 | custom fusion | bytes 4194560 | tf_op jit(solution)/shard_map/gather | solution.py:137
  15.1 0.0 copy-start.1
  15.1 0.0 copy-start.3
  15.1 0.0 copy-start.4
  15.1 7.0 %all-to-all-start.1 = ((bf16[16,4,2,8,1024]{4,3,2,1,0:T(8,128)(2,1)}), bf16[16,4,2,8,1024]{4,3,2,1,0:T(8,128)(2,1)}, u32[]{:S(2)}, u32[]{:S(2)}) async-start(bf16[16,4,2,8,1024]{4,3,2,1,0:T(8,128)(2,1)} %bitcast.14), calls=%async_computation.1 | async-start | bytes 4194304 | tf_op jit(solution)/shard_map/all_to_all | solution.py:138
  22.8 0.0 copy-done.5
  22.9 0.0 copy-done.1
  22.9 0.0 copy-done.3
  22.9 0.0 copy-done.4
  22.9 0.0 copy-start.2
  22.9 1.2 %copy-done.2 = bf16[1,2,256,1024]{3,2,1,0:T(8,128)(2,1)S(1)} copy-done((bf16[1,2,256,1024]{3,2,1,0:T(8,128)(2,1)S(1)}, bf16[1,2,256,1024]{3,2,1,0:T(8,128)(2,1)}, u32[]{:S(2)}) %copy-start.2) | copy-done | bytes 1048600
  24.1 16.8 %local_part.1 = (bf16[4,8,512,128]{3,2,1,0:T(8,128)(2,1)}, f32[4,8,512,128]{3,2,1,0:T(8,128)}, f32[4,8,512,128]{3,2,1,0:T(8,128)}) custom-call(bf16[1,4,64,8192]{3,2,1,0:T(8,128)(2,1)} %q_ref.1, bf16[1,4,2,64,1024]{4,3,2,1,0:T(8,128)(2,1)S(1)} %copy-done.1, bf16[1,2,256,1024]{3,2,1,0:T(8,128)(2,1)S(1)} %copy-done.2, f32[64,128]{1,0:T(8,128)S(1)} %copy-done.4, ...), custom_call_target="tpu_custom_call" | custom-call | flops 2684354560 | bytes 31457280 | tf_op jit(solution)/shard_map/local_part/pallas_call | solution.py:147
  40.9 28.8 %all-to-all-done.1 = bf16[16,4,2,8,1024]{4,3,2,1,0:T(8,128)(2,1)} async-done(((bf16[16,4,2,8,1024]{4,3,2,1,0:T(8,128)(2,1)}), bf16[16,4,2,8,1024]{4,3,2,1,0:T(8,128)(2,1)}, u32[]{:S(2)}, u32[]{:S(2)}) %all-to-all-start.1) | async-done | bytes 2097184 | tf_op jit(solution)/shard_map/all_to_all | solution.py:138
  69.7 24.1 %paged_part.1 = bf16[1,4,64,8192]{3,2,1,0:T(8,128)(2,1)} custom-call(s32[4,16]{1,0:T(4,128)S(1)} %fusion.2.index_ref, s32[1]{0:T(128)S(6)} %copy.24.count_ref, bf16[4,8,512,128]{3,2,1,0:T(8,128)(2,1)} %get-tuple-element.8.rot_ref, f32[4,8,512,128]{3,2,1,0:T(8,128)} %get-tuple-element.9.acc_ref, f32[4,8,512,128]{3,2,1,0:T(8,128)} %get-tuple-element.10.ml_ref, ...), custom_call_target="tpu_custom_call" | custom-call | tf_op jit(solution)/shard_map/paged_part/pallas_call | solution.py:182
  (7 shorter events, 0.1 us)
Async XLA Ops:
  0.0 13.1 %copy-start = (bf16[64,2,8,1024]{3,2,1,0:T(8,128)(2,1)S(1)}, bf16[64,2,8,1024]{3,2,1,0:T(8,128)(2,1)}, u32[]{:S(2)}) copy-start(bf16[64,2,8,1024]{3,2,1,0:T(8,128)(2,1)} %param.12) | copy-start | bytes 6291460
  15.1 7.7 %copy-start.5 = (s32[1,4,16]{2,1,0:T(4,128)S(1)}, s32[1,4,16]{2,1,0:T(4,128)}, u32[]{:S(2)}) copy-start(s32[1,4,16]{2,1,0:T(4,128)} %param.14) | copy-start | bytes 772
  15.1 7.7 %copy-start.1 = (bf16[1,4,2,64,1024]{4,3,2,1,0:T(8,128)(2,1)S(1)}, bf16[1,4,2,64,1024]{4,3,2,1,0:T(8,128)(2,1)}, u32[]{:S(2)}) copy-start(bf16[1,4,2,64,1024]{4,3,2,1,0:T(8,128)(2,1)} %seg_ref.1) | copy-start | bytes 3145732
  15.1 7.8 %copy-start.3 = (f32[64,128]{1,0:T(8,128)S(1)}, f32[64,128]{1,0:T(8,128)}, u32[]{:S(2)}) copy-start(f32[64,128]{1,0:T(8,128)} %constant.56.clone.sin_ref) | copy-start | bytes 98308
  15.1 7.8 %copy-start.4 = (f32[64,128]{1,0:T(8,128)S(1)}, f32[64,128]{1,0:T(8,128)}, u32[]{:S(2)}) copy-start(f32[64,128]{1,0:T(8,128)} %constant.55.clone.cos_ref) | copy-start | bytes 98308
  15.1 54.6 %all-to-all-start.1 = ((bf16[16,4,2,8,1024]{4,3,2,1,0:T(8,128)(2,1)}), bf16[16,4,2,8,1024]{4,3,2,1,0:T(8,128)(2,1)}, u32[]{:S(2)}, u32[]{:S(2)}) async-start(bf16[16,4,2,8,1024]{4,3,2,1,0:T(8,128)(2,1)} %bitcast.14), calls=%async_computation.1 | async-start | bytes 4194304 | tf_op jit(solution)/shard_map/all_to_all | solution.py:138
  22.9 1.2 %copy-start.2 = (bf16[1,2,256,1024]{3,2,1,0:T(8,128)(2,1)S(1)}, bf16[1,2,256,1024]{3,2,1,0:T(8,128)(2,1)}, u32[]{:S(2)}) copy-start(bf16[1,2,256,1024]{3,2,1,0:T(8,128)(2,1)} %prefix_ref.1) | copy-start | bytes 3145732
where the time goes:
time: 94.2 us; the launch traced here: 93.9 us
  Pallas kernels  40.9 us (43%)
  waiting for transfers between devices  28.8 us (31%)
  blocking collectives  10.2 us (11%)
  starting transfers between devices  7.04 us (7%)
  local copies, waits for them, and re-layouts  5.47 us (6%)
    all_to_all x1, waiting for transfers between devices, per_device(): lax.all_to_all(located, 'prob', split_axis=0, concat_axis=0, tiled=True)  28.8 us
    pallas_call x1, Pallas kernels, per_device(): pl.pallas_call(paged_part, grid_spec=grid_spec, out_shape=jax.ShapeDtypeS...  24.1 us
    pallas_call x1, Pallas kernels, per_device(): pl.pallas_call(local_part, grid=(beams,), in_specs=[pl.BlockSpec((1, 1, s...  16.8 us
    all_to_all x1, blocking collectives, per_device(): lax.all_to_all(requests, 'prob', split_axis=0, concat_axis=0, tiled=True)  10.2 us
    all_to_all x1, starting transfers between devices, per_device(): lax.all_to_all(located, 'prob', split_axis=0, concat_axis=0, tiled=True)  7.04 us
    unnamed x13, local copies, waits for them, and re-layouts  2.14 us
    gather x1, local copies, waits for them, and re-layouts, per_device(): page_pool[asked.reshape(-1)]  2 us
  transfers between devices with their start and end apart: 1, of which 1 were waited for; matrix products, arithmetic and copies ran while one was open for 0% of the time, Pallas kernels for 18%

commit v1 on v0

v1 whole, which is shorter than its diff:
```python
import functools
import math

import jax
import jax.numpy as jnp
import numpy as np
from jax import lax
from jax.experimental import pallas as pl
from jax.experimental.pallas import tpu as pltpu
from jax.sharding import PartitionSpec as P

HD = 128
NEG_FILL = -1e30
MESH = pl.DeviceIdType.MESH
UNROLL = 2
LOG2_SCALE = math.log2(math.e) / math.sqrt(HD)


def rotary_tables(length, offset):
    half = HD // 2
    frequency = np.exp(np.arange(half) * (-2.0 * math.log(1000000.0) / HD))
    angles = (np.arange(length) + offset)[:, None] * frequency[None, :]
    cosine, sine = np.cos(angles), np.sin(angles)
    return (
        jnp.asarray(np.concatenate([cosine, cosine], axis=1), jnp.float32),
        jnp.asarray(np.concatenate([-sine, sine], axis=1), jnp.float32),
    )


def rotate(values, cosine, signed_sine):
    floats = values.astype(jnp.float32)
    swapped = pltpu.roll(floats, HD // 2, 1)
    return (floats * cosine + swapped * signed_sine).astype(jnp.bfloat16)


def dot_keys(queries, keys):
    return lax.dot_general(
        queries, keys, (((1,), (1,)), ((), ())), preferred_element_type=jnp.float32
    )


def dot_values(weights, values):
    extended = jnp.concatenate([values, jnp.ones_like(values)], axis=1)
    return jnp.dot(weights, extended, preferred_element_type=jnp.float32)


def exchange_and_attend(
    n, q_hbm, seg_hbm, prefix_hbm, pool_hbm, slots_ref, cos_ref, sin_ref, version_ref, count_ref,
    out_hbm,
    q_ref, seg_ref, prefix_ref, pool_ref, asked_ref, asked_smem, stage_ref, page_ref,
    rot_ref, acc_ref, max_ref, sum_ref, key_ref, value_ref,
    load_sem, ask_send, ask_recv, ask_sem, page_send, page_recv, out_sem,
):
    myself = lax.axis_index("prob")
    beams, seg_len, model_width = q_ref.shape
    kv_heads = rot_ref.shape[1]
    group = model_width // HD // kv_heads
    rows = group * seg_len
    rounds, capacity = stage_ref.shape[:2]
    pages = version_ref.shape[2]
    page_len = pool_ref.shape[1] // 2
    remote = [r for r in range(rounds) if (r + 1) % n]

    loads = [
        pltpu.make_async_copy(source, target, load_sem.at[i])
        for i, (source, target) in enumerate(
            (
                (pool_hbm, pool_ref),
                (prefix_hbm.at[0], prefix_ref),
                (seg_hbm.at[0], seg_ref),
                (q_hbm.at[0], q_ref),
            )
        )
    ]
    for load in loads:
        load.start()

    shifts = sorted({(1 + r) % n for r in remote} | {(-1 - r) % n for r in remote})
    barrier = pltpu.get_barrier_semaphore()
    for shift in shifts:
        pl.semaphore_signal(
            barrier, inc=1, device_id={"prob": lax.rem(myself + shift, n)}, device_id_type=MESH
        )
    pl.semaphore_wait(barrier, len(shifts))

    def ask(r):
        return pltpu.make_async_remote_copy(
            src_ref=slots_ref.at[r],
            dst_ref=asked_ref.at[r],
            send_sem=ask_send.at[r],
            recv_sem=ask_recv.at[r],
            device_id={"prob": lax.rem(myself + (1 + r) % n, n)},
            device_id_type=MESH,
        )

    def serve(r):
        return pltpu.make_async_remote_copy(
            src_ref=stage_ref.at[r],
            dst_ref=page_ref.at[r],
            send_sem=page_send.at[r],
            recv_sem=page_recv.at[r],
            device_id={"prob": lax.rem(myself + (-1 - r) % n, n)},
            device_id_type=MESH,
        )

    for r in remote:
        ask(r).start()
    for r in range(rounds):
        if r not in remote:
            asked_ref[r] = slots_ref[r]
    loads[0].wait()
    for r in remote:
        ask(r).wait_recv()
    table = pltpu.make_async_copy(asked_ref, asked_smem, ask_sem)
    table.start()
    table.wait()
    for r in sorted(range(rounds), key=lambda r: -min((r + 1) % n, (-1 - r) % n)):
        for c in range(capacity):
            page = pool_ref[asked_smem[r, 0, c]]
            if r in remote:
                stage_ref[r, c] = page
            else:
                page_ref[r, c] = page
        if r in remote:
            serve(r).start()
    for load in loads[1:]:
        load.wait()

    cosine, sine = cos_ref[...], sin_ref[...]
    token = lax.broadcasted_iota(jnp.int32, (group, seg_len, seg_len), 1).reshape(rows, seg_len)
    causal = token >= lax.broadcasted_iota(jnp.int32, (rows, seg_len), 1)

    def column(number):
        return pl.ds(pl.multiple_of(number * HD, HD), HD)

    def local_step(step, carry):
        beam, head = step // kv_heads, step % kv_heads
        queries = jnp.concatenate(
            [
                rotate(q_ref[beam, :, column(head * group + g)], cosine, sine)
                for g in range(group)
            ],
            axis=0,
        )
        fresh_keys = rotate(seg_ref[beam, 0, :, column(head)], cosine, sine)
        prefix_scores = dot_keys(queries, prefix_ref[0, :, column(head)])
        fresh_scores = jnp.where(causal, dot_keys(queries, fresh_keys), NEG_FILL)
        row_max = jnp.maximum(
            prefix_scores.max(-1, keepdims=True), fresh_scores.max(-1, keepdims=True)
        )
        shift = row_max * LOG2_SCALE
        prefix_exp = jnp.exp2(prefix_scores * LOG2_SCALE - shift).astype(jnp.bfloat16)
        fresh_exp = jnp.exp2(fresh_scores * LOG2_SCALE - shift).astype(jnp.bfloat16)
        mixed = dot_values(prefix_exp, prefix_ref[1, :, column(head)]) + dot_values(
            fresh_exp, seg_ref[beam, 1, :, column(head)]
        )
        rot_ref[beam, head] = queries
        acc_ref[beam, head] = mixed[:, :HD]
        sum_ref[beam, head] = mixed[:, HD:]
        max_ref[beam, head] = jnp.broadcast_to(shift, (rows, HD))
        return carry

    lax.fori_loop(0, beams * kv_heads, local_step, 0)

    for r in remote:
        serve(r).wait_recv()

    def store(beam):
        return pltpu.make_async_copy(q_ref.at[beam], out_hbm.at[0, beam], out_sem.at[beam])

    def beam_step(beam, carry):
        live = beam < count_ref[0]

        def fetched(j):
            number = j * beams + version_ref[0, beam, j]
            page = page_ref[lax.rem(number, n), lax.div(number, n)].astype(jnp.float32)
            return page[:page_len], page[page_len:]

        for j in range(0, pages, 2):
            first, second = fetched(j), fetched(j + 1)
            span = pl.ds(j * page_len, 2 * page_len)
            key_ref[span] = jnp.concatenate([first[0], second[0]], axis=0).astype(jnp.bfloat16)
            value_ref[span] = jnp.concatenate([first[1], second[1]], axis=0).astype(jnp.bfloat16)

        def head_step(head):
            scores = dot_keys(rot_ref[beam, head], key_ref[:, column(head)]) * LOG2_SCALE
            old_shift = max_ref[beam, head]
            shift = jnp.maximum(old_shift, scores.max(-1, keepdims=True))
            weights = jnp.exp2(scores - shift[:, :1]).astype(jnp.bfloat16)
            decay = jnp.exp2(old_shift - shift)
            mixed = dot_values(weights, value_ref[:, column(head)])
            total = mixed[:, HD:] + sum_ref[beam, head] * decay
            result = (mixed[:, :HD] + acc_ref[beam, head] * decay) / total
            result = jnp.where(live, result, 0.0).astype(jnp.bfloat16)
            for g in range(group):
                q_ref[beam, :, column(head * group + g)] = result[g * seg_len : (g + 1) * seg_len]

        def heads_step(step, inner):
            for k in range(UNROLL):
                head_step(step * UNROLL + k)
            return inner

        lax.fori_loop(0, kv_heads // UNROLL, heads_step, 0)
        store(beam).start()
        return carry

    lax.fori_loop(0, beams, beam_step, 0)
    for beam in range(beams):
        store(beam).wait()
    for r in remote:
        ask(r).wait_send()
        serve(r).wait_send()


def per_device(
    segment_queries, segment_kv, prefix_kv, page_pool, beam_count, page_version, page_slot
):
    devices = lax.axis_size("prob")
    _, beams, seg_len, model_width = segment_queries.shape
    shared = prefix_kv.shape[2]
    pool_pages, _, page_len, kv_width = page_pool.shape
    context_pages = page_version.shape[2]
    kv_heads = kv_width // HD
    rows = model_width // kv_width * seg_len
    rounds = min(devices, pool_pages)
    capacity = (pool_pages + devices - 1) // devices
    cosine, sine = rotary_tables(seg_len, shared + context_pages * page_len)
    slots = page_slot.reshape(-1)
    slots = jnp.pad(slots, (0, capacity * rounds - slots.shape[0]))
    slots = slots.reshape(capacity, rounds).T[:, None, :]
    slots = jnp.pad(slots, ((0, 0), (0, 0), (0, HD - capacity)))

    any_spec = pl.BlockSpec(memory_space=pl.ANY)
    vmem_spec = pl.BlockSpec(memory_space=pltpu.VMEM)
    smem_spec = pl.BlockSpec(memory_space=pltpu.SMEM)
    page_block = (rounds, capacity, 2 * page_len, kv_width)
    state = (beams, kv_heads, rows, HD)
    dma = pltpu.SemaphoreType.DMA
    positions = shared + seg_len + context_pages * page_len
    return pl.pallas_call(
        functools.partial(exchange_and_attend, devices),
        in_specs=[any_spec] * 4 + [vmem_spec] * 3 + [smem_spec] * 2,
        out_specs=any_spec,
        out_shape=jax.ShapeDtypeStruct(segment_queries.shape, jnp.bfloat16),
        scratch_shapes=[
            pltpu.VMEM(segment_queries.shape[1:], jnp.bfloat16),
            pltpu.VMEM(segment_kv.shape[1:], jnp.bfloat16),
            pltpu.VMEM(prefix_kv.shape[1:], jnp.bfloat16),
            pltpu.VMEM((pool_pages, 2 * page_len, kv_width), jnp.bfloat16),
            pltpu.VMEM((rounds, 1, HD), jnp.int32),
            pltpu.SMEM((rounds, 1, HD), jnp.int32),
            pltpu.VMEM(page_block, jnp.bfloat16),
            pltpu.VMEM(page_block, jnp.bfloat16),
            pltpu.VMEM(state, jnp.bfloat16),
            pltpu.VMEM(state, jnp.float32),
            pltpu.VMEM(state, jnp.float32),
            pltpu.VMEM(state, jnp.float32),
            pltpu.VMEM((context_pages * page_len, kv_width), jnp.bfloat16),
            pltpu.VMEM((context_pages * page_len, kv_width), jnp.bfloat16),
            dma((4,)),
            dma((rounds,)),
            dma((rounds,)),
            dma(()),
            dma((rounds,)),
            dma((rounds,)),
            dma((beams,)),
        ],
        compiler_params=pltpu.CompilerParams(
            collective_id=0, has_side_effects=True, vmem_limit_bytes=56 * 1024 * 1024
        ),
        cost_estimate=pl.CostEstimate(
            flops=4 * beams * kv_heads * rows * HD * positions,
            bytes_accessed=14 * 1024 * 1024,
            transcendentals=beams * kv_heads * rows * positions,
        ),
        name="exchange_and_attend",
    )(
        segment_queries,
        segment_kv,
        prefix_kv,
        page_pool.reshape(pool_pages, 2 * page_len, kv_width),
        slots,
        cosine,
        sine,
        page_version,
        beam_count,
    )


def solution(mesh):
    placed = (
        P(("groups", "prob"), None, None, None),
        P(("groups", "prob"), None, None, None, None),
        P(("groups", "prob"), None, None, None),
        P(("groups", "prob"), None, None, None),
        P(("groups", "prob")),
        P(("groups", "prob"), None, None),
        P(("groups", "prob"), None, None),
    )
    return jax.shard_map(
        per_device,
        mesh=mesh,
        in_specs=placed,
        out_specs=P(("groups", "prob"), None, None, None),
        check_vma=False,
    )
```

time: 94.2 us -> 80.9 us (0.86)
  the two profiles are of different devices: /device:TPU:11 before, /device:TPU:0 now
where the time goes in v1:
time: 80.9 us; the launch traced here: 80.3 us
  Pallas kernels  73.4 us (91%)
  local copies, waits for them, and re-layouts  6.17 us (8%)
    pallas_call x1, Pallas kernels, per_device(): pl.pallas_call(functools.partial(exchange_and_attend, devices), in_specs=...  73.4 us
    unnamed x2, local copies, waits for them, and re-layouts  5.4 us

profile of v1, /device:TPU:0, one launch (start us, length us, event | category | flops | bytes accessed | tf_op | source)
XLA Modules:
  0.0 80.3 jit_solution(7657151832226077210)
XLA Ops:
  0.7 0.8 copy.12
  1.4 0.1 reshape.9
  1.5 0.1 copy.13
  1.6 0.6 pad.4.slots_ref
  2.2 73.4 %exchange_and_attend.1 = bf16[1,4,64,8192]{3,2,1,0:T(8,128)(2,1)} custom-call(bf16[1,4,64,8192]{3,2,1,0:T(8,128)(2,1)} %q_hbm.1, bf16[1,4,2,64,1024]{4,3,2,1,0:T(8,128)(2,1)} %seg_hbm.1, bf16[1,2,256,1024]{3,2,1,0:T(8,128)(2,1)} %prefix_hbm.1, bf16[64,16,1024]{2,1,0:T(8,128)(2,1)} %bitcast.5, s32[16,1,128]{2,1,0:T(1,128)} %pad.4.slots_ref, ...), custom_call_target="tpu_custom_call" | custom-call | flops 3758096384 | bytes 14680064 | tf_op jit(solution)/shard_map/exchange_and_attend/pallas_call | solution.py:240
  75.6 4.6 %copy.16 = bf16[1,4,64,8192]{3,2,1,0:T(8,128)(2,1)} copy(bf16[1,4,64,8192]{3,2,1,0:T(8,128)(2,1)} %exchange_and_attend.1) | data formatting | bytes 8388608

commit v2 on v1

--- a/solution.py
+++ b/solution.py
@@ -58,6 +58,7 @@
     rows = group * seg_len
     rounds, capacity = stage_ref.shape[:2]
     pages = version_ref.shape[2]
+    copies = slots_ref.shape[1]
     page_len = pool_ref.shape[1] // 2
     remote = [r for r in range(rounds) if (r + 1) % n]
 
@@ -85,7 +86,7 @@
 
     def ask(r):
         return pltpu.make_async_remote_copy(
-            src_ref=slots_ref.at[r],
+            src_ref=slots_ref,
             dst_ref=asked_ref.at[r],
             send_sem=ask_send.at[r],
             recv_sem=ask_recv.at[r],
@@ -107,16 +108,16 @@
         ask(r).start()
     for r in range(rounds):
         if r not in remote:
-            asked_ref[r] = slots_ref[r]
+            asked_ref[r] = slots_ref[...]
     loads[0].wait()
     for r in remote:
         ask(r).wait_recv()
     table = pltpu.make_async_copy(asked_ref, asked_smem, ask_sem)
     table.start()
     table.wait()
-    for r in sorted(range(rounds), key=lambda r: -min((r + 1) % n, (-1 - r) % n)):
+    for r in sorted(range(rounds), key=lambda r: (r % beams, -min((r + 1) % n, (-1 - r) % n))):
         for c in range(capacity):
-            page = pool_ref[asked_smem[r, 0, c]]
+            page = pool_ref[asked_smem[r, 0, min(r + c * n, copies - 1)]]
             if r in remote:
                 stage_ref[r, c] = page
             else:
@@ -162,18 +163,23 @@
 
     lax.fori_loop(0, beams * kv_heads, local_step, 0)
 
-    for r in remote:
-        serve(r).wait_recv()
-
     def store(beam):
         return pltpu.make_async_copy(q_ref.at[beam], out_hbm.at[0, beam], out_sem.at[beam])
 
-    def beam_step(beam, carry):
+    def beam_step(beam):
         live = beam < count_ref[0]
+        for r in remote:
+            if r % beams == beam:
+                serve(r).wait_recv()
 
         def fetched(j):
-            number = j * beams + version_ref[0, beam, j]
-            page = page_ref[lax.rem(number, n), lax.div(number, n)].astype(jnp.float32)
+            version = version_ref[0, beam, j]
+            page = None
+            for candidate in range(beam + 1):
+                number = j * beams + candidate
+                stored = page_ref[number % n, number // n]
+                page = stored if page is None else jnp.where(version == candidate, stored, page)
+            page = page.astype(jnp.float32)
             return page[:page_len], page[page_len:]
 
         for j in range(0, pages, 2):
@@ -202,9 +208,9 @@
 
         lax.fori_loop(0, kv_heads // UNROLL, heads_step, 0)
         store(beam).start()
-        return carry
-
-    lax.fori_loop(0, beams, beam_step, 0)
+
+    for beam in range(beams):
+        beam_step(beam)
     for beam in range(beams):
         store(beam).wait()
     for r in remote:
@@ -225,10 +231,7 @@
     rounds = min(devices, pool_pages)
     capacity = (pool_pages + devices - 1) // devices
     cosine, sine = rotary_tables(seg_len, shared + context_pages * page_len)
-    slots = page_slot.reshape(-1)
-    slots = jnp.pad(slots, (0, capacity * rounds - slots.shape[0]))
-    slots = slots.reshape(capacity, rounds).T[:, None, :]
-    slots = jnp.pad(slots, ((0, 0), (0, 0), (0, HD - capacity)))
+    slots = page_slot.reshape(1, pool_pages)
 
     any_spec = pl.BlockSpec(memory_space=pl.ANY)
     vmem_spec = pl.BlockSpec(memory_space=pltpu.VMEM)
@@ -247,8 +250,8 @@
             pltpu.VMEM(segment_kv.shape[1:], jnp.bfloat16),
             pltpu.VMEM(prefix_kv.shape[1:], jnp.bfloat16),
             pltpu.VMEM((pool_pages, 2 * page_len, kv_width), jnp.bfloat16),
-            pltpu.VMEM((rounds, 1, HD), jnp.int32),
-            pltpu.SMEM((rounds, 1, HD), jnp.int32),
+            pltpu.VMEM((rounds, 1, pool_pages), jnp.int32),
+            pltpu.SMEM((rounds, 1, pool_pages), jnp.int32),
             pltpu.VMEM(page_block, jnp.bfloat16),
             pltpu.VMEM(page_block, jnp.bfloat16),
             pltpu.VMEM(state, jnp.bfloat16),

time: 80.9 us -> 69.5 us (0.86)
  Pallas kernels: 73.4 us -> 62.6 us
    pallas_call x1, Pallas kernels: 73.4 us -> 62.6 us  [per_device(): pl.pallas_call(functools.partial(exchange_and_attend, devices), in_specs=...]
where the time goes in v2:
time: 69.5 us; the launch traced here: 69.3 us
  Pallas kernels  62.6 us (90%)
  local copies, waits for them, and re-layouts  6 us (9%)
    pallas_call x1, Pallas kernels, per_device(): pl.pallas_call(functools.partial(exchange_and_attend, devices), in_specs=...  62.6 us
    unnamed x2, local copies, waits for them, and re-layouts  5.4 us

profile of v2, /device:TPU:0, one launch (start us, length us, event | category | flops | bytes accessed | tf_op | source)
XLA Modules:
  0.0 69.3 jit_solution(4419288683961586392)
XLA Ops:
  0.7 0.8 %copy.11 = s32[1,16,4]{2,1,0:T(8,128)S(1)} copy(s32[1,16,4]{1,2,0:T(4,128)} %param.15) | data formatting | bytes 512 | tf_op args[6]
  1.4 0.6 reshape.7.slots_ref
  2.0 62.6 %exchange_and_attend.1 = bf16[1,4,64,8192]{3,2,1,0:T(8,128)(2,1)} custom-call(bf16[1,4,64,8192]{3,2,1,0:T(8,128)(2,1)} %q_hbm.1, bf16[1,4,2,64,1024]{4,3,2,1,0:T(8,128)(2,1)} %seg_hbm.1, bf16[1,2,256,1024]{3,2,1,0:T(8,128)(2,1)} %prefix_hbm.1, bf16[64,16,1024]{2,1,0:T(8,128)(2,1)} %bitcast.1, s32[1,64]{1,0:T(1,128)} %reshape.7.slots_ref, ...), custom_call_target="tpu_custom_call" | custom-call | flops 3758096384 | bytes 14680064 | tf_op jit(solution)/shard_map/exchange_and_attend/pallas_call | solution.py:243
  64.6 4.6 %copy.14 = bf16[1,4,64,8192]{3,2,1,0:T(8,128)(2,1)} copy(bf16[1,4,64,8192]{3,2,1,0:T(8,128)(2,1)} %exchange_and_attend.1) | data formatting | bytes 8388608

commit v3 on v2

--- a/solution.py
+++ b/solution.py
@@ -46,10 +46,10 @@
 
 def exchange_and_attend(
     n, q_hbm, seg_hbm, prefix_hbm, pool_hbm, slots_ref, cos_ref, sin_ref, version_ref, count_ref,
-    out_hbm,
+    out_hbm, rot_hbm, acc_hbm, max_hbm, sum_hbm, key_hbm, value_hbm,
     q_ref, seg_ref, prefix_ref, pool_ref, asked_ref, asked_smem, stage_ref, page_ref,
     rot_ref, acc_ref, max_ref, sum_ref, key_ref, value_ref,
-    load_sem, ask_send, ask_recv, ask_sem, page_send, page_recv, out_sem,
+    load_sem, ask_send, ask_recv, ask_sem, page_send, page_recv, out_sem, state_sem,
 ):
     myself = lax.axis_index("prob")
     beams, seg_len, model_width = q_ref.shape
@@ -162,6 +162,22 @@
         return carry
 
     lax.fori_loop(0, beams * kv_heads, local_step, 0)
+    last = beams - 1
+    state = [
+        pltpu.make_async_copy(source, target, state_sem.at[i])
+        for i, (source, target) in enumerate(
+            (
+                (rot_ref.at[last], rot_hbm),
+                (acc_ref.at[last], acc_hbm),
+                (max_ref.at[last], max_hbm),
+                (sum_ref.at[last], sum_hbm),
+                (key_ref, key_hbm),
+                (value_ref, value_hbm),
+            )
+        )
+    ]
+    for copy in state[:4]:
+        copy.start()
 
     def store(beam):
         return pltpu.make_async_copy(q_ref.at[beam], out_hbm.at[0, beam], out_sem.at[beam])
@@ -187,6 +203,11 @@
             span = pl.ds(j * page_len, 2 * page_len)
             key_ref[span] = jnp.concatenate([first[0], second[0]], axis=0).astype(jnp.bfloat16)
             value_ref[span] = jnp.concatenate([first[1], second[1]], axis=0).astype(jnp.bfloat16)
+
+        if beam == last:
+            for copy in state[4:]:
+                copy.start()
+            return
 
         def head_step(head):
             scores = dot_keys(rot_ref[beam, head], key_ref[:, column(head)]) * LOG2_SCALE
@@ -211,11 +232,66 @@
 
     for beam in range(beams):
         beam_step(beam)
-    for beam in range(beams):
+    for beam in range(last):
         store(beam).wait()
+    for copy in state:
+        copy.wait()
     for r in remote:
         ask(r).wait_send()
         serve(r).wait_send()
+
+
+def last_beam(
+    count_ref, done_hbm, rot_ref, acc_ref, max_ref, sum_ref, key_ref, value_ref,
+    out_hbm, out_ref, done_sem, out_sem,
+):
+    step = pl.program_id(0)
+    steps = pl.num_programs(0)
+    done = done_hbm.shape[1]
+    seg_len = out_ref.shape[1]
+    heads, rows = rot_ref.shape[:2]
+    group = rows // seg_len
+    width = out_ref.shape[2]
+    live = done < count_ref[0]
+
+    def forward(beam):
+        return pltpu.make_async_copy(done_hbm.at[0, beam], out_hbm.at[0, beam], done_sem.at[beam])
+
+    def store(number):
+        start = number * width
+        if not isinstance(number, int):
+            start = pl.multiple_of(start, HD)
+        return pltpu.make_async_copy(
+            out_ref.at[number], out_hbm.at[0, done, :, pl.ds(start, width)], out_sem.at[number]
+        )
+
+    @pl.when(step == 0)
+    def _():
+        for beam in range(done):
+            forward(beam).start()
+
+    for head in range(heads):
+        columns = slice(head * HD, (head + 1) * HD)
+        scores = dot_keys(rot_ref[head], key_ref[:, columns]) * LOG2_SCALE
+        old_shift = max_ref[head]
+        shift = jnp.maximum(old_shift, scores.max(-1, keepdims=True))
+        weights = jnp.exp2(scores - shift[:, :1]).astype(jnp.bfloat16)
+        decay = jnp.exp2(old_shift - shift)
+        mixed = dot_values(weights, value_ref[:, columns])
+        total = mixed[:, HD:] + sum_ref[head] * decay
+        result = (mixed[:, :HD] + acc_ref[head] * decay) / total
+        result = jnp.where(live, result, 0.0).astype(jnp.bfloat16)
+        for g in range(group):
+            place = (head * group + g) * HD
+            out_ref[step, :, place : place + HD] = result[g * seg_len : (g + 1) * seg_len]
+    store(step).start()
+
+    @pl.when(step == steps - 1)
+    def _():
+        for beam in range(done):
+            forward(beam).wait()
+        for number in range(out_ref.shape[0]):
+            store(number).wait()
 
 
 def per_device(
@@ -240,11 +316,20 @@
     state = (beams, kv_heads, rows, HD)
     dma = pltpu.SemaphoreType.DMA
     positions = shared + seg_len + context_pages * page_len
-    return pl.pallas_call(
+    span = (context_pages * page_len, kv_width)
+    finished, *partial = pl.pallas_call(
         functools.partial(exchange_and_attend, devices),
         in_specs=[any_spec] * 4 + [vmem_spec] * 3 + [smem_spec] * 2,
-        out_specs=any_spec,
-        out_shape=jax.ShapeDtypeStruct(segment_queries.shape, jnp.bfloat16),
+        out_specs=[any_spec] * 7,
+        out_shape=[
+            jax.ShapeDtypeStruct((1, beams - 1, seg_len, model_width), jnp.bfloat16),
+            jax.ShapeDtypeStruct(state[1:], jnp.bfloat16),
+            jax.ShapeDtypeStruct(state[1:], jnp.float32),
+            jax.ShapeDtypeStruct(state[1:], jnp.float32),
+            jax.ShapeDtypeStruct(state[1:], jnp.float32),
+            jax.ShapeDtypeStruct(span, jnp.bfloat16),
+            jax.ShapeDtypeStruct(span, jnp.bfloat16),
+        ],
         scratch_shapes=[
             pltpu.VMEM(segment_queries.shape[1:], jnp.bfloat16),
             pltpu.VMEM(segment_kv.shape[1:], jnp.bfloat16),
@@ -267,6 +352,7 @@
             dma((rounds,)),
             dma((rounds,)),
             dma((beams,)),
+            dma((6,)),
         ],
         compiler_params=pltpu.CompilerParams(
             collective_id=0, has_side_effects=True, vmem_limit_bytes=56 * 1024 * 1024
@@ -288,6 +374,23 @@
         page_version,
         beam_count,
     )
+    steps = kv_heads // UNROLL
+    head_spec = pl.BlockSpec((UNROLL, rows, HD), lambda i: (i, 0, 0))
+    page_spec = pl.BlockSpec((span[0], UNROLL * HD), lambda i: (0, i))
+    return pl.pallas_call(
+        last_beam,
+        grid=(steps,),
+        in_specs=[smem_spec, any_spec] + [head_spec] * 4 + [page_spec] * 2,
+        out_specs=any_spec,
+        out_shape=jax.ShapeDtypeStruct(segment_queries.shape, jnp.bfloat16),
+        scratch_shapes=[
+            pltpu.VMEM((steps, seg_len, model_width // steps), jnp.bfloat16),
+            dma((beams,)),
+            dma((steps,)),
+        ],
+        compiler_params=pltpu.CompilerParams(vmem_limit_bytes=60 * 1024 * 1024),
+        name="last_beam",
+    )(beam_count, finished, *partial)
 
 
 def solution(mesh):

time: 69.5 us -> 159 us (2.29)
  Pallas kernels: 62.6 us -> 156 us
  local copies, waits for them, and re-layouts: 6 us -> 1.36 us
    pallas_call x0 -> x1, Pallas kernels: none -> 97.9 us  [per_device(): pl.pallas_call(last_beam, grid=(steps,), in_specs=[smem_spec, any_spec] +...]
    unnamed x2 -> x1, local copies, waits for them, and re-layouts: 5.4 us -> 0.76 us
    pallas_call x1, Pallas kernels: 62.6 us -> 58.6 us  [per_device(): pl.pallas_call(functools.partial(exchange_and_attend, devices), in_specs=...]
where the time goes in v3:
time: 159 us
  Pallas kernels  156 us (98%)
    pallas_call x1, Pallas kernels, per_device(): pl.pallas_call(last_beam, grid=(steps,), in_specs=[smem_spec, any_spec] +...  97.9 us
    pallas_call x1, Pallas kernels, per_device(): pl.pallas_call(functools.partial(exchange_and_attend, devices), in_specs=...  58.6 us

profile of v3, /device:TPU:0, one launch (start us, length us, event | category | flops | bytes accessed | tf_op | source)
XLA Modules:
  0.0 158.5 jit_solution(12669061971821448835)
XLA Ops:
  0.7 0.8 copy.11
  1.4 0.6 reshape.7.slots_ref
  2.0 58.6 %exchange_and_attend.1 = (bf16[1,3,64,8192]{3,2,1,0:T(8,128)(2,1)}, bf16[8,512,128]{2,1,0:T(8,128)(2,1)}, f32[8,512,128]{2,1,0:T(8,128)}, f32[8,512,128]{2,1,0:T...) custom-call(bf16[1,4,64,8192]{3,2,1,0:T(8,128)(2,1)} %q_hbm.1, ...), custom_call_target="tpu_custom_call" | custom-call | flops 3758096384 | bytes 14680064 | tf_op jit(solution)/shard_map/exchange_and_attend/pallas_call | solution.py:320
  60.6 97.9 %last_beam.1 = bf16[1,4,64,8192]{3,2,1,0:T(8,128)(2,1)} custom-call(s32[1]{0:T(128)S(6)} %copy.12.count_ref, bf16[1,3,64,8192]{3,2,1,0:T(8,128)(2,1)} %get-tuple-element.12.done_hbm, bf16[8,512,128]{2,1,0:T(8,128)(2,1)} %get-tuple-element.13.rot_ref, f32[8,512,128]{2,1,0:T(8,128)} %get-tuple-element.14.acc_ref, f32[8,512,128]{2,1,0:T(8,128)} %get-tuple-element.15.max_ref, ...), custom_call_target="tpu_custom_call" | custom-call | tf_op jit(solution)/shard_map/last_beam/pallas_call | solution.py:380

commit v4 on v3

--- a/solution.py
+++ b/solution.py
@@ -243,7 +243,7 @@
 
 def last_beam(
     count_ref, done_hbm, rot_ref, acc_ref, max_ref, sum_ref, key_ref, value_ref,
-    out_hbm, out_ref, done_sem, out_sem,
+    out_hbm, out_ref, done_ref, fetch_sem, done_sem, out_sem,
 ):
     step = pl.program_id(0)
     steps = pl.num_programs(0)
@@ -254,8 +254,11 @@
     width = out_ref.shape[2]
     live = done < count_ref[0]
 
+    def fetch(beam):
+        return pltpu.make_async_copy(done_hbm.at[0, beam], done_ref.at[beam], fetch_sem.at[beam])
+
     def forward(beam):
-        return pltpu.make_async_copy(done_hbm.at[0, beam], out_hbm.at[0, beam], done_sem.at[beam])
+        return pltpu.make_async_copy(done_ref.at[beam], out_hbm.at[0, beam], done_sem.at[beam])
 
     def store(number):
         start = number * width
@@ -268,6 +271,12 @@
     @pl.when(step == 0)
     def _():
         for beam in range(done):
+            fetch(beam).start()
+
+    @pl.when(step == 1)
+    def _():
+        for beam in range(done):
+            fetch(beam).wait()
             forward(beam).start()
 
     for head in range(heads):
@@ -385,6 +394,8 @@
         out_shape=jax.ShapeDtypeStruct(segment_queries.shape, jnp.bfloat16),
         scratch_shapes=[
             pltpu.VMEM((steps, seg_len, model_width // steps), jnp.bfloat16),
+            pltpu.VMEM((beams - 1, seg_len, model_width), jnp.bfloat16),
+            dma((beams,)),
             dma((beams,)),
             dma((steps,)),
         ],

time: 159 us -> 68.8 us (0.43)
  Pallas kernels: 156 us -> 66.5 us
    pallas_call x1, Pallas kernels: 97.9 us -> 7.91 us  [per_device(): pl.pallas_call(last_beam, grid=(steps,), in_specs=[smem_spec, any_spec] +...]
where the time goes in v4:
time: 68.8 us; the launch traced here: 68.5 us
  Pallas kernels  66.5 us (97%)
  local copies, waits for them, and re-layouts  1.36 us (2%)
    pallas_call x1, Pallas kernels, per_device(): pl.pallas_call(functools.partial(exchange_and_attend, devices), in_specs=...  58.6 us
    pallas_call x1, Pallas kernels, per_device(): pl.pallas_call(last_beam, grid=(steps,), in_specs=[smem_spec, any_spec] +...  7.91 us

profile of v4, /device:TPU:0, one launch (start us, length us, event | category | flops | bytes accessed | tf_op | source)
XLA Modules:
  0.0 68.5 jit_solution(8364768865745912232)
XLA Ops:
  0.7 0.8 %copy.11 = s32[1,16,4]{2,1,0:T(8,128)S(1)} copy(s32[1,16,4]{1,2,0:T(4,128)} %param.15) | data formatting | bytes 512 | tf_op args[6]
  1.4 0.6 reshape.7.slots_ref
  2.0 58.6 %exchange_and_attend.1 = (bf16[1,3,64,8192]{3,2,1,0:T(8,128)(2,1)}, bf16[8,512,128]{2,1,0:T(8,128)(2,1)}, f32[8,512,128]{2,1,0:T(8,128)}, f32[8,512,128]{2,1,0:T...) custom-call(bf16[1,4,64,8192]{3,2,1,0:T(8,128)(2,1)} %q_hbm.1, ...), custom_call_target="tpu_custom_call" | custom-call | flops 3758096384 | bytes 14680064 | tf_op jit(solution)/shard_map/exchange_and_attend/pallas_call | solution.py:329
  60.6 7.9 %last_beam.1 = bf16[1,4,64,8192]{3,2,1,0:T(8,128)(2,1)} custom-call(s32[1]{0:T(128)S(6)} %copy.12.count_ref, bf16[1,3,64,8192]{3,2,1,0:T(8,128)(2,1)} %get-tuple-element.12.done_hbm, bf16[8,512,128]{2,1,0:T(8,128)(2,1)} %get-tuple-element.13.rot_ref, f32[8,512,128]{2,1,0:T(8,128)} %get-tuple-element.14.acc_ref, f32[8,512,128]{2,1,0:T(8,128)} %get-tuple-element.15.max_ref, ...), custom_call_target="tpu_custom_call" | custom-call | tf_op jit(solution)/shard_map/last_beam/pallas_call | solution.py:389
